TPU v7x, 32 devices: a whole 2x2x4 slice. The times are simulated.
32 devices in a mesh: orb: 8 (over y, x, core), ao: 4 (over z).
Axes of the slice: x: 2, y: 2, z: 4, core: 2. Of those that a mesh axis runs over, the one named last changes fastest.
Arguments:
- coeff: float32 [2, 8, 64, 80, 128], P(None, 'orb', 'ao')
- metric_coeff: float32 [2, 8, 64, 80, 128], P(None, 'orb', 'ao')
- tile_list: int32 [2, 8, 64], P(None, 'orb', 'ao'), may hold values from 0 to 191, as said below
- tile_atoms: int32 [192, 128], replicated, may hold values from 0 to 7, never falling along the last dimension, each value on 1 to 32 neighbouring positions
Outputs:
- coeff_out: float32 [2, 8, 64, 80, 128], P(None, 'orb', 'ao')
- metric_out: float32 [2, 8, 64, 80, 128], P(None, 'orb', 'ao')
Inputs may be any that keep to these rules, and one draw needn't show every extreme that they name: `tile_list`: within one block the ids are distinct, and an id at list position k leaves the remainder k // 16 when divided by 4. `tile_atoms`: along a tile's atomic orbitals the slot never falls, and each of the 8 slots holds 1 to 32 atomic orbitals.
All inputs are finite; a program needn't handle non-finite values.
Results may differ from a plain program's by a relative error of at most 0.0003.
Values sent between devices are 32-bit elements; how exact they have to be, the bound alone decides.
No kernel may reach another device: no remote copies, remote signals or barrier semaphores. Data moves between devices by JAX's collectives and lax.ppermute only.
A program may use at most 64 MiB of HBM per device.

v0:
```python
import functools

import jax
import jax.numpy as jnp
from jax import lax
from jax.experimental import pallas as pl
from jax.experimental.pallas import tpu as pltpu
from jax.sharding import PartitionSpec as P

ATOMS = 8
LANES = 128
STEP_LENGTH = 3.0
EPSILON = 1e-12
CONVERGED = 1.2e-7
SOME_VMEM = 20_000_000

F32 = jnp.float32
BF16 = jnp.bfloat16
NT = (((1,), (1,)), ((), ()))
NN = (((1,), (0,)), ((), ()))
HBM = pl.BlockSpec(memory_space=pltpu.HBM)
VMEM = pl.BlockSpec(memory_space=pltpu.VMEM)


def halves(value):
    high = value.astype(BF16)
    return high, (value - high.astype(F32)).astype(BF16)


def dot(left, right, dims):
    return lax.dot_general(left, right, dims, preferred_element_type=F32)


def stacked_dot(left, right, rows, dims):
    wide = dot(left, right[0], dims)
    return wide[:rows] + (wide[rows:] + dot(left[:rows], right[1], dims))


def packed_rows(orbitals):
    pieces = -(-orbitals // (LANES - orbitals))
    tail = 2 * orbitals // (pieces + 1) // 8 * 8
    return 2 * orbitals - tail, tail, pieces


def pack(value, orbitals):
    keep, tail, pieces = packed_rows(orbitals)
    spare = LANES - orbitals
    lane = lax.broadcasted_iota(jnp.int32, (tail, LANES), 1)
    moved = [
        jnp.where(lane >= orbitals, pltpu.roll(value[keep:], (orbitals - i * spare) % LANES, 1), 0.0)
        for i in range(pieces)
    ]
    if keep > pieces * tail:
        moved.append(jnp.zeros((keep - pieces * tail, LANES), F32))
    return value[:keep] + jnp.concatenate(moved, axis=0)


def unpack(value, orbitals):
    keep, tail, pieces = packed_rows(orbitals)
    spare = LANES - orbitals
    lane = lax.broadcasted_iota(jnp.int32, (keep, LANES), 1)
    moved = jnp.where(lane >= orbitals, value, 0.0)
    last = sum(
        pltpu.roll(moved[i * tail : (i + 1) * tail], (i * spare - orbitals) % LANES, 1) for i in range(pieces)
    )
    return jnp.concatenate([jnp.where(lane < orbitals, value, 0.0), last], axis=0)


def crosses(position, last):
    return ((position % 4 == 3) & (position < last)) | ((position % 4 == 0) & (position > 0))


class Blocks:
    def __init__(self, first_round, refs, buffer, lists, sems, count, orbitals):
        self.count, self.orbitals, self.buffer, self.lists, self.sems = count, orbitals, buffer, lists, sems
        self.first_round, self.refs = first_round, refs

    def copy(self, slot, part, source):
        target = self.lists.at[slot] if part == 2 else self.buffer.at[slot, part]
        return pltpu.make_async_copy(source, target, self.sems.at[slot, part])

    def start(self):
        rows = self.count * self.orbitals
        if self.first_round:
            tile_list, coeff, metric = self.refs
            for slot in (1, 0):
                for part, source in ((2, tile_list), (0, coeff), (1, metric)):
                    self.copy(slot, part, source.at[slot]).start()
            return
        own_coeff, own_metric, even, odd_metric, relayed, rebuilt = self.refs
        position, last = lax.axis_index("orb"), lax.axis_size("orb") - 1
        odd = position % 2 == 1
        across = crosses(position, last)

        def begin(condition, slot, coeff, metric, metric_row):
            note_row = 2 * rows if metric_row else rows

            @pl.when(condition)
            def _():
                self.copy(slot, 2, coeff.at[pl.ds(note_row, 8)]).start()
                self.copy(slot, 0, coeff.at[pl.ds(0, rows)]).start()
                self.copy(slot, 1, metric.at[pl.ds(metric_row, rows)]).start()

        for slot, from_even, end in ((1, jnp.logical_not(odd), last), (0, odd, 0)):
            from_odd = jnp.logical_not(from_even) & (position != end)
            begin(from_even, slot, even, even, rows)
            begin(position == end, slot, own_coeff, own_metric, 0)
            begin(from_odd & across, slot, relayed, odd_metric, 0)
            begin(from_odd & jnp.logical_not(across), slot, rebuilt, odd_metric, 0)

    def wait(self, slot):
        for part in (2, 0, 1):
            if self.first_round:
                source = self.refs[0 if part == 2 else 1].at[slot]
            else:
                source = self.refs[0].at[pl.ds(0, 8 if part == 2 else self.count * self.orbitals)]
            self.copy(slot, part, source).wait()

    def tile(self, slot, k):
        return self.lists[slot, 0, k].astype(jnp.int32)

    def value(self, slot, c, k):
        return self.buffer[slot, c, k * self.orbitals : (k + 1) * self.orbitals, :]

    def wide(self, slot, c, k):
        return jnp.concatenate([self.value(slot, c, k), self.value(slot, c, k + 1)], axis=1)

    def place(self, slot, k):
        entry, place = self.tile(slot, k), jnp.int32(self.count)
        for l in range(self.count):
            place = jnp.where(entry == self.tile(1 - slot, l), jnp.int32(l), place)
        return place


def own_rows(slot, orbitals):
    return slice(slot * orbitals, (slot + 1) * orbitals)


def lanes_at(k, tiles=1):
    if isinstance(k, int):
        return slice(k * LANES, (k + tiles) * LANES)
    return pl.ds(pl.multiple_of(k * LANES, LANES), tiles * LANES)


def clear_spare(slot, blocks, arrays):
    for array in arrays:
        for c in range(2):
            array[slot, c, own_rows(slot, blocks.orbitals), blocks.count * LANES :] = jnp.zeros(
                (blocks.orbitals, LANES), BF16
            )


def carry(blocks, arrays):
    for slot in range(2):
        rows = own_rows(1 - slot, blocks.orbitals)
        for k in range(blocks.count):
            here, there = lanes_at(k), lanes_at(blocks.place(slot, k))
            for array in arrays:
                for c in range(2):
                    array[slot, c, rows, here] = array[1 - slot, c, rows, there]


def gradient_kernel(first_round, count, orbitals, sources, atoms_hbm, *refs):
    inputs, refs = refs[:sources], refs[sources:]
    out_ref, right_high, right_rest, buffer, lists, sems, atoms_ref, atoms_sem, left = refs
    blocks = Blocks(first_round, inputs, buffer, lists, sems, count, orbitals)
    atoms_copy = pltpu.make_async_copy(atoms_hbm, atoms_ref, atoms_sem)
    atoms_copy.start()
    blocks.start()
    width, gap = count * LANES, LANES - orbitals
    chunk = min(8, count)
    slots = lax.broadcasted_iota(jnp.int32, (ATOMS, LANES), 0)
    blank = jnp.zeros((ATOMS, LANES), F32)
    lane = lax.broadcasted_iota(jnp.int32, (orbitals, count * ATOMS), 1) // (2 * ATOMS)
    atoms_copy.wait()

    for slot in (1, 0):
        blocks.wait(slot)
        clear_spare(slot, blocks, (right_high, right_rest))
        rows = own_rows(slot, orbitals)
        member = []
        for k in range(count):
            one = (atoms_ref[pl.ds(blocks.tile(slot, k), 1), :] == slots).astype(F32)
            member.append(jnp.concatenate([blank, one] if k % 2 else [one, blank], axis=1))
        member = jnp.concatenate(member, axis=0).astype(BF16)
        member_wide = jnp.concatenate([member, member], axis=1)
        member_tall = jnp.concatenate([member, member], axis=0)

        for first in range(0, count, chunk):
            pairs = range(0, chunk, 2)
            coeffs = jnp.concatenate([blocks.wide(slot, 0, first + k) for k in pairs], axis=0)
            metric = jnp.concatenate([blocks.wide(slot, 1, first + k) for k in pairs], axis=0)
            charges = dot(jnp.concatenate(halves(coeffs * metric), axis=1), member_wide, NT)
            charges = jnp.concatenate(
                [
                    jnp.where(lane == first // 2 + j, charges[j * orbitals : (j + 1) * orbitals], 0.0)
                    for j in range(len(pairs))
                ],
                axis=0,
            )
            spread = dot(jnp.concatenate(halves(charges), axis=1), member_tall, NN)
            for c, value in enumerate((coeffs, metric)):
                weighted, plain = halves(value * spread), halves(value)
                for j, k in enumerate(pairs):
                    picked, here = slice(j * orbitals, (j + 1) * orbitals), lanes_at(first + k, 2)
                    left[slot, c, :orbitals, here] = weighted[0][picked]
                    left[slot, c, orbitals:, here] = weighted[1][picked]
                    right_high[slot, c, rows, here] = plain[0][picked]
                    right_rest[slot, c, rows, here] = plain[1][picked]


    carry(blocks, (right_high, right_rest))
    fill_lanes = jnp.zeros((2 * orbitals, gap), F32)
    fill_rows = jnp.zeros((gap, LANES), F32)
    products = []
    for slot in range(2):
        wide = sum(dot(right_high[slot, 1 - c, :, :width], left[slot, c], NT) for c in range(2))
        rest = sum(dot(right_rest[slot, 1 - c, :, :width], left[slot, c, :orbitals], NT) for c in range(2))
        value = jnp.concatenate([wide[:, :orbitals] + (wide[:, orbitals:] + rest), fill_lanes], axis=1)
        products.append(
            [jnp.concatenate([value[own_rows(i, orbitals)], fill_rows], axis=0) for i in range(2)]
        )
    (upper, upper_lower), (lower_upper, lower) = products
    row = lax.broadcasted_iota(jnp.int32, (LANES, LANES), 0)
    column = lax.broadcasted_iota(jnp.int32, (LANES, LANES), 1)
    diagonal = jnp.where(column > row, upper.T - upper, jnp.where(column < row, lower.T - lower, 0.0))
    cross = upper_lower.T - lower_upper
    packed = pack(jnp.concatenate([2.0 * diagonal[:orbitals], 2.0 * cross[:orbitals]], axis=0), orbitals)
    for z in range(out_ref.shape[0]):
        out_ref[z] = packed

def norm_kernel(parts_ref, packed_ref, norm_ref):
    packed = parts_ref[0]
    for z in range(1, parts_ref.shape[0]):
        packed = packed + parts_ref[z]
    packed_ref[...] = packed
    total = jnp.broadcast_to(2.0 * jnp.sum(packed * packed, keepdims=True), norm_ref.shape[1:])
    for g in range(norm_ref.shape[0]):
        norm_ref[g] = total


def compact(turn, orbitals):
    lane = lax.broadcasted_iota(jnp.int32, turn.shape, 1)
    turn = jnp.where(lane < LANES, turn, 0.0) + pltpu.roll(
        jnp.where(lane >= LANES, turn, 0.0), LANES + orbitals, 1
    )
    return halves(turn[:, : 2 * orbitals])


def later_slot(position):
    return jnp.where((position % 2 == 0) & (position != 0), 0, 1)


def note_of(tile, count):
    lane = lax.broadcasted_iota(jnp.int32, (8, LANES), 1)
    ids = jnp.zeros((8, LANES), jnp.int32)
    for k in range(count):
        ids = jnp.where(lane == k, tile(k), ids)
    return ids.astype(F32)


def apply(turn_ref, slot, c, data_high, data_rest, count, orbitals, put):
    chunk = min(4, count)
    for first in range(0, count, chunk):
        here = lanes_at(first, chunk)
        value = stacked_dot(
            turn_ref[slot], (data_high[slot, c, :, here], data_rest[slot, c, :, here]), orbitals, NN
        )
        for j in range(chunk):
            put(slice((first + j) * orbitals, (first + j + 1) * orbitals), value[:, lanes_at(j)])


def later_kernel(count, orbitals, turn_ref, data_high, data_rest, list_hbm, out_ref, lists, list_sem):
    rows = count * orbitals
    list_copy = pltpu.make_async_copy(list_hbm, lists, list_sem)
    list_copy.start()
    slot = later_slot(lax.axis_index("orb"))
    for c in range(2):

        def put(place, value, c=c):
            out_ref[c * rows + place.start : c * rows + place.stop, :] = value

        apply(turn_ref, slot, c, data_high, data_rest, count, orbitals, put)
    list_copy.wait()
    out_ref[2 * rows :] = note_of(lambda k: lists[slot, 0, k], count)


def rotation_kernel(first_round, count, orbitals, groups, *refs):
    norm_ref, packed_ref, data_high, data_rest = refs[:4]
    final = not first_round
    if first_round:
        list_hbm, odd_coeff, odd_metric, rows_ref, turn_ref, lists, list_sem, power_ref, total_ref = refs[4:]
        list_copy = pltpu.make_async_copy(list_hbm, lists, list_sem)
        list_copy.start()
    else:
        outs, (result, out_sems, power_ref, total_ref, turn_ref) = refs[4:6], refs[6:]
    size, wide, gap = 2 * orbitals, 2 * LANES, LANES - orbitals
    rows = count * orbitals

    squares = norm_ref[0]
    for g in range(1, groups):
        squares = squares + norm_ref[g]
    scale = (STEP_LENGTH / jnp.sqrt(squares / groups + EPSILON))[:1, :]
    row = lax.broadcasted_iota(jnp.int32, (LANES, LANES), 0)
    column = lax.broadcasted_iota(jnp.int32, (LANES, LANES), 1)
    fill = jnp.zeros((gap, LANES), F32)
    scaled = unpack(packed_ref[...], orbitals) * (-0.5 * scale)
    diagonal = jnp.concatenate([scaled[:orbitals], fill], axis=0)
    cross = jnp.concatenate([scaled[orbitals:], fill], axis=0)
    above = jnp.where(column > row, diagonal, 0.0)
    below = jnp.where(column < row, diagonal, 0.0)
    generator = jnp.concatenate(
        [
            jnp.concatenate([(above - above.T)[:orbitals], cross[:orbitals]], axis=1),
            jnp.concatenate([-cross.T[:orbitals], (below - below.T)[:orbitals]], axis=1),
        ],
        axis=0,
    )
    big_row = lax.broadcasted_iota(jnp.int32, (size, wide), 0)
    big_column = lax.broadcasted_iota(jnp.int32, (size, wide), 1)
    identity = (big_column == jnp.where(big_row < orbitals, big_row, big_row + gap)).astype(F32)

    def spaced(value):
        blank = jnp.zeros((gap, wide), value.dtype)
        return jnp.concatenate([value[:orbitals], blank, value[orbitals:], blank], axis=0)

    def times(left, right):
        high, rest = halves(right)
        return stacked_dot(
            jnp.concatenate(halves(left), axis=0), (spaced(high), spaced(rest)), left.shape[0], NN
        )

    square = -times(generator, generator)
    bound = jnp.sqrt(0.5 * jnp.sum(square * square, keepdims=True))
    centre = 1.0 + 0.5 * bound
    radius = 0.5 * bound / centre
    power_ref[...] = radius * identity - square * (1.0 / centre)
    total_ref[...] = identity + generator

    def more(radius):
        power, total = power_ref[...], total_ref[...]
        product = times(jnp.concatenate([total, power], axis=0), power)
        total_ref[...] = total + product[:size]
        power_ref[...] = product[size:]
        return radius * radius

    lax.while_loop(lambda radius: radius > CONVERGED, more, jnp.max(radius))
    turn = total_ref[...] * (2.0 / centre) - identity
    turn_high, turn_rest = compact(turn, orbitals)
    for slot in range(2):
        mine = own_rows(slot, orbitals)
        turn_ref[slot, :orbitals] = turn_high[mine]
        turn_ref[slot, orbitals:] = turn_rest[mine]

    if final:
        stores = []
        for slot in range(2):
            for c in range(2):

                def put(place, value, slot=slot, c=c):
                    result[slot, c, place, :] = value

                apply(turn_ref, slot, c, data_high, data_rest, count, orbitals, put)
                stores.append(
                    pltpu.make_async_copy(result.at[slot, c], outs[c].at[slot], out_sems.at[slot, c])
                )
                stores[-1].start()
        for copy in stores:
            copy.wait()
        return
    slot = 1 - later_slot(lax.axis_index("orb"))
    total_ref[...] = turn
    odd_rows = pl.ds(pl.multiple_of(slot * orbitals, 8), orbitals)
    rows_ref[8 : 8 + orbitals] = total_ref[odd_rows, :LANES]
    rows_ref[8 + orbitals :] = total_ref[odd_rows, LANES:]
    list_copy.wait()
    row = lax.broadcasted_iota(jnp.int32, (8, LANES), 0)
    notes = [note_of(lambda k, i=i: lists[i, 0, k], count) for i in range(2)]
    rows_ref[:8] = jnp.where(row == 0, notes[0], notes[1])
    odd_coeff[rows:] = jnp.where(slot == 0, notes[0], notes[1])
    for c, out_ref in enumerate((odd_coeff, odd_metric)):

        def put(place, value, out_ref=out_ref):
            out_ref[place, :] = value

        apply(turn_ref, slot, c, data_high, data_rest, count, orbitals, put)


def crossing_kernel(count, orbitals, raw_hbm, turn_hbm, out_ref, *refs):
    buffer, lists, turn_ref, note, result, sems, out_sems = refs[:7]
    data_high, data_rest, other_high, other_rest = refs[7:]
    position, last = lax.axis_index("orb"), lax.axis_size("orb") - 1
    rows, width = count * orbitals, count * LANES

    @pl.when(((position % 4 == 1) & (position < last)) | (position % 4 == 2))
    def _():
        wanted = position % 2
        loads = [pltpu.make_async_copy(turn_hbm.at[pl.ds(0, 8)], lists, sems.at[0, 0])]
        for i, block in enumerate((wanted, 1 - wanted)):
            first = pl.multiple_of(8 + block * orbitals, 8)
            loads.append(pltpu.make_async_copy(raw_hbm.at[block], buffer.at[i], sems.at[i, 1]))
            loads.append(
                pltpu.make_async_copy(turn_hbm.at[pl.ds(first, orbitals)], turn_ref.at[i], sems.at[i, 2])
            )
        for copy in loads:
            copy.start()
        for copy in loads:
            copy.wait()
        for k in range(count):
            here, mine = lanes_at(k), slice(k * orbitals, (k + 1) * orbitals)
            high, rest = halves(buffer[0, mine, :])
            data_high[:orbitals, here] = high
            data_rest[:orbitals, here] = rest
            high, rest = halves(buffer[1, mine, :])
            other_high[:, here] = high
            other_rest[:, here] = rest
        other_high[:, width:] = jnp.zeros((orbitals, LANES), BF16)
        other_rest[:, width:] = jnp.zeros((orbitals, LANES), BF16)
        for k in range(count):
            entry, place = lists[wanted, k], jnp.int32(count)
            for l in range(count):
                place = jnp.where(entry == lists[1 - wanted, l], jnp.int32(l), place)
            here, there = lanes_at(k), lanes_at(place)
            data_high[orbitals:, here] = other_high[:, there]
            data_rest[orbitals:, here] = other_rest[:, there]
        note[...] = note_of(lambda k: lists[wanted, k].astype(jnp.int32), count)
        stores = [
            pltpu.make_async_copy(note, out_ref.at[pl.ds(rows, 8)], out_sems.at[0]),
            pltpu.make_async_copy(result, out_ref.at[pl.ds(0, rows)], out_sems.at[1]),
        ]
        stores[0].start()
        turn = jnp.concatenate(compact(jnp.concatenate([turn_ref[0], turn_ref[1]], axis=1), orbitals), axis=0)
        chunk = min(4, count)
        for first in range(0, count, chunk):
            here = lanes_at(first, chunk)
            value = stacked_dot(turn, (data_high[:, here], data_rest[:, here]), orbitals, NN)
            for j in range(chunk):
                k = first + j
                result[k * orbitals : (k + 1) * orbitals, :] = value[:, lanes_at(j)]
        stores[1].start()
        for copy in stores:
            copy.wait()


def swap(block, pairs):
    return lax.ppermute(block, "orb", both_ways(pairs))


def both_ways(pairs):
    return [pair for k in pairs for pair in ((k, k + 1), (k + 1, k))]


def shards(coeff, metric_coeff, tile_list, tile_atoms):
    groups, parts = lax.axis_size("orb"), lax.axis_size("ao")
    _, _, count, orbitals, lanes = coeff.shape
    rows, size, width = count * orbitals, 2 * orbitals, count * lanes
    keep = packed_rows(orbitals)[0]
    dma = pltpu.SemaphoreType.DMA
    inner = range(1, groups - 1, 2)
    direct = [k for k in inner if k % 4 != 3]
    across = [k for k in inner if k % 4 == 3]
    carried = jax.ShapeDtypeStruct((2, 2, size, width + lanes), BF16)

    def call(kernel, name, vmem, out_shape, scratch, *operands, specs=None, out_specs=None, cost=None):
        return pl.pallas_call(
            kernel,
            out_shape=out_shape,
            in_specs=specs or [HBM] * len(operands),
            out_specs=out_specs or [HBM] * len(out_shape),
            scratch_shapes=scratch,
            compiler_params=pltpu.CompilerParams(vmem_limit_bytes=vmem),
            cost_estimate=cost,
            name=name,
        )(*operands)

    def shaped(*shape):
        return jax.ShapeDtypeStruct(shape, F32)

    inputs = (tile_list, coeff.reshape(2, rows, lanes), metric_coeff.reshape(2, rows, lanes))
    inputs = tuple(pltpu.with_memory_space_constraint(array, pltpu.HBM) for array in inputs)
    tile_atoms = pltpu.with_memory_space_constraint(tile_atoms, pltpu.HBM)
    raw = swap(inputs[1], direct)
    for first_round in (True, False):
        final = not first_round
        loading = [
            pltpu.VMEM((2, 2, rows, lanes), F32),
            pltpu.SMEM((2, 1, count), jnp.int32) if first_round else pltpu.SMEM((2, 8, lanes), F32),
            dma((2, 3)),
        ]
        gradient, *split = call(
            functools.partial(gradient_kernel, first_round, count, orbitals, len(inputs)),
            "gradient",
            SOME_VMEM,
            (shaped(parts, keep, lanes), carried, carried),
            loading
            + [
                pltpu.VMEM(tile_atoms.shape, jnp.int32),
                dma,
                pltpu.VMEM((2, 2, size, width), BF16),
            ],
            tile_atoms,
            *inputs,
            out_specs=(VMEM,) * 3,
        )
        gathered = lax.all_to_all(gradient, "ao", 0, 0)
        packed, norms = call(
            norm_kernel,
            "norm",
            SOME_VMEM,
            (shaped(keep, lanes), shaped(groups, 8, lanes)),
            [],
            gathered,
            specs=[VMEM],
            out_specs=(VMEM, VMEM),
        )
        if first_round:
            norms, raw = lax.optimization_barrier((norms, raw))
        norms = lax.all_to_all(norms, "orb", 0, 0)
        squares = [pltpu.VMEM((size, 2 * lanes), F32)] * 2
        listing = [pltpu.SMEM((2, 1, count), jnp.int32), dma]
        turns = jax.ShapeDtypeStruct((2, size, size), BF16)
        kernel = functools.partial(rotation_kernel, first_round, count, orbitals, groups)
        if final:
            outs = call(
                kernel,
                "rotation",
                SOME_VMEM,
                (shaped(2, rows, lanes),) * 2,
                [pltpu.VMEM((2, 2, rows, lanes), F32), dma((2, 2)), *squares, pltpu.VMEM(turns.shape, BF16)],
                norms,
                packed,
                *split,
                specs=[VMEM] * 4,
            )
            return tuple(out.reshape(coeff.shape) for out in outs)
        odd_coeff, odd_metric, turn, turns = call(
            kernel,
            "rotation",
            SOME_VMEM,
            (shaped(rows + 8, lanes), shaped(rows, lanes), shaped(8 + size, lanes), turns),
            listing + squares,
            norms,
            packed,
            *split,
            inputs[0],
            specs=[VMEM] * 4 + [HBM],
            out_specs=[VMEM] * 4,
        )
        halfway = lax.ppermute(
            odd_coeff, "orb", [route for k in across for route in ((k, k + 4), (k + 1, k - 3))]
        )
        got_turn = swap(turn, direct)
        got_metric = swap(odd_metric, inner)
        turns, got_turn = lax.optimization_barrier((turns, got_turn))
        (even,) = call(
            functools.partial(later_kernel, count, orbitals),
            "later",
            SOME_VMEM,
            (shaped(2 * rows + 8, lanes),),
            listing,
            turns,
            *split,
            inputs[0],
            specs=[VMEM] * 3 + [HBM],
            out_specs=[VMEM],
        )
        got_even = swap(even, range(0, groups, 2))
        relayed = lax.ppermute(
            halfway, "orb", [route for k in across for route in ((k + 4, k + 1), (k - 3, k))]
        )
        half = pltpu.VMEM((orbitals, width + lanes), BF16)
        (rebuilt,) = call(
            functools.partial(crossing_kernel, count, orbitals),
            "crossing",
            SOME_VMEM,
            (shaped(rows + 8, lanes),),
            [
                pltpu.VMEM((2, rows, lanes), F32),
                pltpu.SMEM((8, lanes), F32),
                pltpu.VMEM((2, orbitals, lanes), F32),
                pltpu.VMEM((8, lanes), F32),
                pltpu.VMEM((rows, lanes), F32),
                dma((2, 3)),
                dma((2,)),
                pltpu.VMEM((size, width), BF16),
                pltpu.VMEM((size, width), BF16),
                half,
                half,
            ],
            raw,
            got_turn,
            cost=pl.CostEstimate(flops=2000 * orbitals * size * width, bytes_accessed=16 * rows * lanes, transcendentals=0),
        )
        inputs = (odd_coeff, odd_metric, got_even, got_metric, relayed, rebuilt)


def solution(mesh):
    blocks = P(None, "orb", "ao", None, None)
    return jax.shard_map(
        shards,
        mesh=mesh,
        in_specs=(blocks, blocks, P(None, "orb", "ao"), P()),
        out_specs=(blocks, blocks),
        check_vma=False,
    )
```

profile of v0, /device:TPU:0, one launch (start us, length us, event | category | flops | bytes accessed | tf_op | source)
XLA Modules:
  0.0 82.1 jit_solution(8841123099879597566)
XLA Ops:
  0.6 0.7 collective-permute-start
  1.4 4.8 %gradient.2 = (f32[4,112,128]{2,1,0:T(8,128)S(1)}, bf16[2,2,160,2176]{3,2,1,0:T(8,128)(2,1)S(1)}, bf16[2,2,160,2176]{3,2,1,0:T(8,128)(2,1)S(1)}) custom-call(s32[192,128]{1,0:T(8,128)} %atoms_hbm.3, s32[2,1,16]{2,1,0:T(1,128)} %list_hbm.1, f32[2,1280,128]{2,1,0:T(8,128)} %bitcast.10, f32[2,1280,128]{2,1,0:T(8,128)} %bitcast.8), custom_call_target="tpu_custom_call" | custom-call | tf_op jit(solution)/shard_map/gradient/pallas_call | solution.py:465
  6.2 13.1 %all_to_all.20.parts_ref = f32[4,112,128]{2,1,0:T(8,128)S(1)} all-to-all(f32[4,112,128]{2,1,0:T(8,128)S(1)} %get-tuple-element.22), channel_id=1, replica_groups=mesh['orb'=8,'ao'=4] {'ao'}, dimensions={0} | all-to-all | bytes 458752 | tf_op jit(solution)/shard_map/all_to_all | solution.py:505
  19.2 0.1 norm.2
  19.4 0.0 collective-permute-done.raw_hbm
  19.4 0.0 copy-start
  19.4 10.2 %all_to_all.21.refs_0_ = f32[8,8,128]{2,1,0:T(8,128)S(1)} all-to-all(f32[8,8,128]{2,1,0:T(8,128)S(1)} %get-tuple-element.24), channel_id=1, replica_groups=mesh['orb'=8,'ao'=4] {'orb'}, dimensions={0} | all-to-all | bytes 65536 | tf_op jit(solution)/shard_map/all_to_all | solution.py:518
  29.6 1.9 %rotation.2 = (f32[1288,128]{1,0:T(8,128)S(1)}, f32[1280,128]{1,0:T(8,128)S(1)}, f32[168,128]{1,0:T(8,128)S(1)}, bf16[2,160,160]{2,1,0:T(8,128)(2,1)S(1)}) custom-call(f32[8,8,128]{2,1,0:T(8,128)S(1)} %all_to_all.21.refs_0_, f32[112,128]{1,0:T(8,128)S(1)} %get-tuple-element.25.refs_1_, bf16[2,2,160,2176]{3,2,1,0:T(8,128)(2,1)S(1)} %get-tuple-element.26.refs_2_.data_high, ...), custom_call_target="tpu_custom_call" | custom-call | tf_op jit(solution)/shard_map/rotation/pallas_call | solution.py:465
  31.5 0.0 copy-done
  31.5 1.3 %collective-permute-start.4 = (f32[1288,128]{1,0:T(8,128)S(1)}, f32[1288,128]{1,0:T(8,128)S(1)}, u32[]{:S(2)}, u32[]{:S(2)}) collective-permute-start(f32[1288,128]{1,0:T(8,128)S(1)} %get-tuple-element.28.refs_0_), channel_id=1, source_target_pairs={{12,28},{16,0},{13,29},{17,1},{14,30},{18,2},{15,31},{19,3}} | collective-permute-start | bytes 1978376 | tf_op jit(solution)/shard_map/ppermute | solution.py:549
  32.8 0.7 collective-permute-start.1
  33.5 0.7 collective-permute-start.3
  34.2 0.0 collective-permute-done.1.turn_hbm
  34.2 0.7 later.1
  34.9 4.2 %collective-permute-start.2 = (f32[2568,128]{1,0:T(8,128)S(1)}, f32[2568,128]{1,0:T(8,128)S(1)}, u32[]{:S(2)}, u32[]{:S(2)}) collective-permute-start(f32[2568,128]{1,0:T(8,128)S(1)} %later.1), channel_id=1, source_target_pairs={{0,4},{4,0},{8,12},{12,8},{16,20},{20,16},{24,28},{28,24},{1,5},{5... | collective-permute-start | bytes 3944456 | tf_op jit(solution)/shard_map/ppermute | solution.py:446
  39.1 4.9 %collective-permute-done.4 = f32[1288,128]{1,0:T(8,128)S(1)} collective-permute-done((f32[1288,128]{1,0:T(8,128)S(1)}, f32[1288,128]{1,0:T(8,128)S(1)}, u32[]{:S(2)}, u32[]{:S(2)}) %collective-permute-start.4) | collective-permute-done | bytes 659488 | tf_op jit(solution)/shard_map/ppermute | solution.py:549
  44.0 1.3 %collective-permute-start.5 = (f32[1288,128]{1,0:T(8,128)S(1)}, f32[1288,128]{1,0:T(8,128)S(1)}, u32[]{:S(2)}, u32[]{:S(2)}) collective-permute-start(f32[1288,128]{1,0:T(8,128)S(1)} %collective-permute-done.4), channel_id=1, source_target_pairs={{28,16},{0,12},{29,17},{1,13},{30,18},{2,14},{31,19},{3,15}} | collective-permute-start | bytes 1978376 | tf_op jit(solution)/shard_map/ppermute | solution.py:568
  45.4 0.1 crossing.1.refs_5_
  45.5 0.0 collective-permute-done.3.refs_3_
  45.5 8.0 %collective-permute-done.5.refs_4_ = f32[1288,128]{1,0:T(8,128)S(1)} collective-permute-done((f32[1288,128]{1,0:T(8,128)S(1)}, f32[1288,128]{1,0:T(8,128)S(1)}, u32[]{:S(2)}, u32[]{:S(2)}) %collective-permute-start.5) | collective-permute-done | bytes 659488 | tf_op jit(solution)/shard_map/ppermute | solution.py:568
  53.4 0.0 collective-permute-done.2.refs_2_
  53.4 4.5 %gradient.3 = (f32[4,112,128]{2,1,0:T(8,128)S(1)}, bf16[2,2,160,2176]{3,2,1,0:T(8,128)(2,1)S(1)}, bf16[2,2,160,2176]{3,2,1,0:T(8,128)(2,1)S(1)}) custom-call(s32[192,128]{1,0:T(8,128)} %atoms_hbm.3, f32[1288,128]{1,0:T(8,128)S(1)} %get-tuple-element.28.refs_0_, f32[1280,128]{1,0:T(8,128)S(1)} %get-tuple-element.29.refs_1_, ...), custom_call_target="tpu_custom_call" | custom-call | tf_op jit(solution)/shard_map/gradient/pallas_call | solution.py:465
  57.9 13.3 %all_to_all.22.parts_ref = f32[4,112,128]{2,1,0:T(8,128)S(1)} all-to-all(f32[4,112,128]{2,1,0:T(8,128)S(1)} %get-tuple-element.35), channel_id=1, replica_groups=mesh['orb'=8,'ao'=4] {'ao'}, dimensions={0} | all-to-all | bytes 458752 | tf_op jit(solution)/shard_map/all_to_all | solution.py:505
  71.2 0.1 norm.3
  71.3 7.2 %all_to_all.23.refs_0_ = f32[8,8,128]{2,1,0:T(8,128)S(1)} all-to-all(f32[8,8,128]{2,1,0:T(8,128)S(1)} %get-tuple-element.36), channel_id=1, replica_groups=mesh['orb'=8,'ao'=4] {'orb'}, dimensions={0} | all-to-all | bytes 65536 | tf_op jit(solution)/shard_map/all_to_all | solution.py:518
  78.6 3.5 %rotation.3 = (f32[2,1280,128]{2,1,0:T(8,128)}, f32[2,1280,128]{2,1,0:T(8,128)}) custom-call(f32[8,8,128]{2,1,0:T(8,128)S(1)} %all_to_all.23.refs_0_, f32[112,128]{1,0:T(8,128)S(1)} %get-tuple-element.37.refs_1_, bf16[2,2,160,2176]{3,2,1,0:T(8,128)(2,1)S(1)} %get-tuple-element.38.refs_2_, bf16[2,2,160,2176]{3,2,1,0:T(8,128)(2,1)S(1)} %get-tuple-element.39.refs_3_), custom_call_target="tpu_custom_call" | custom-call | tf_op jit(solution)/shard_map/rotation/pallas_call | solution.py:465
Async XLA Ops:
  0.6 18.7 %collective-permute-start = (f32[2,1280,128]{2,1,0:T(8,128)}, f32[2,1280,128]{2,1,0:T(8,128)S(1)}, u32[]{:S(2)}, u32[]{:S(2)}) collective-permute-start(f32[2,1280,128]{2,1,0:T(8,128)} %bitcast.9), channel_id=1, source_target_pairs={{4,8},{8,4},{20,24},{24,20},{5,9},{9,5},{21,25},{25,21},{6,10},{10... | collective-permute-start | bytes 3932168 | tf_op jit(solution)/shard_map/ppermute | solution.py:446
  19.4 12.1 %copy-start = (f32[2,1280,128]{2,1,0:T(8,128)}, f32[2,1280,128]{2,1,0:T(8,128)S(1)}, u32[]{:S(2)}) copy-start(f32[2,1280,128]{2,1,0:T(8,128)S(1)} %collective-permute-done.raw_hbm) | copy-start | bytes 3932164
  31.5 12.5 %collective-permute-start.4 = (f32[1288,128]{1,0:T(8,128)S(1)}, f32[1288,128]{1,0:T(8,128)S(1)}, u32[]{:S(2)}, u32[]{:S(2)}) collective-permute-start(f32[1288,128]{1,0:T(8,128)S(1)} %get-tuple-element.28.refs_0_), channel_id=1, source_target_pairs={{12,28},{16,0},{13,29},{17,1},{14,30},{18,2},{15,31},{19,3}} | collective-permute-start | bytes 1978376 | tf_op jit(solution)/shard_map/ppermute | solution.py:549
  32.8 1.4 %collective-permute-start.1 = (f32[168,128]{1,0:T(8,128)S(1)}, f32[168,128]{1,0:T(8,128)S(1)}, u32[]{:S(2)}, u32[]{:S(2)}) collective-permute-start(f32[168,128]{1,0:T(8,128)S(1)} %get-tuple-element.31), channel_id=1, source_target_pairs={{4,8},{8,4},{20,24},{24,20},{5,9},{9,5},{21,25},{25,21},{6,10},{10... | collective-permute-start | bytes 258056 | tf_op jit(solution)/shard_map/ppermute | solution.py:446
  33.5 12.0 %collective-permute-start.3 = (f32[1280,128]{1,0:T(8,128)S(1)}, f32[1280,128]{1,0:T(8,128)S(1)}, u32[]{:S(2)}, u32[]{:S(2)}) collective-permute-start(f32[1280,128]{1,0:T(8,128)S(1)} %get-tuple-element.29.refs_1_), channel_id=1, source_target_pairs={{4,8},{8,4},{12,16},{16,12},{20,24},{24,20},{5,9},{9,5},{13,17},{1... | collective-permute-start | bytes 1966088 | tf_op jit(solution)/shard_map/ppermute | solution.py:446
  34.9 18.5 %collective-permute-start.2 = (f32[2568,128]{1,0:T(8,128)S(1)}, f32[2568,128]{1,0:T(8,128)S(1)}, u32[]{:S(2)}, u32[]{:S(2)}) collective-permute-start(f32[2568,128]{1,0:T(8,128)S(1)} %later.1), channel_id=1, source_target_pairs={{0,4},{4,0},{8,12},{12,8},{16,20},{20,16},{24,28},{28,24},{1,5},{5... | collective-permute-start | bytes 3944456 | tf_op jit(solution)/shard_map/ppermute | solution.py:446
  44.0 9.4 %collective-permute-start.5 = (f32[1288,128]{1,0:T(8,128)S(1)}, f32[1288,128]{1,0:T(8,128)S(1)}, u32[]{:S(2)}, u32[]{:S(2)}) collective-permute-start(f32[1288,128]{1,0:T(8,128)S(1)} %collective-permute-done.4), channel_id=1, source_target_pairs={{28,16},{0,12},{29,17},{1,13},{30,18},{2,14},{31,19},{3,15}} | collective-permute-start | bytes 1978376 | tf_op jit(solution)/shard_map/ppermute | solution.py:568
where the time goes:
time: 82.5 us; the launch traced here: 82.1 us
  blocking collectives  43.7 us (53%)
  Pallas kernels  15.8 us (19%)
  waiting for transfers between devices  12.9 us (16%)
  starting transfers between devices  8.91 us (11%)
    all_to_all x2, blocking collectives, shards(): gathered = lax.all_to_all(gradient, 'ao', 0, 0)  26.3 us
    all_to_all x2, blocking collectives, shards(): norms = lax.all_to_all(norms, 'orb', 0, 0)  17.4 us
    pallas_call x8, Pallas kernels, call(): pl.pallas_call(kernel, out_shape=out_shape, in_specs=specs or [HBM] * len...  15.8 us
    ppermute x1, waiting for transfers between devices, shards(): lax.ppermute(halfway, 'orb', [route for k in across for route in ((k + 4,...  7.98 us
    ppermute x4, starting transfers between devices, swap(): return lax.ppermute(block, 'orb', both_ways(pairs))  6.29 us
    ppermute x1, waiting for transfers between devices, shards(): lax.ppermute(odd_coeff, 'orb', [route for k in across for route in ((k, k...  4.89 us
  transfers between devices with their start and end apart: 6, of which 2 were waited for; matrix products, arithmetic and copies ran while one was open for 0% of the time, Pallas kernels for 7%

commit v1 on v0

--- a/solution.py
+++ b/solution.py
@@ -168,7 +168,7 @@
     atoms_copy.start()
     blocks.start()
     width, gap = count * LANES, LANES - orbitals
-    chunk = min(8, count)
+    chunk = min(16, count)
     slots = lax.broadcasted_iota(jnp.int32, (ATOMS, LANES), 0)
     blank = jnp.zeros((ATOMS, LANES), F32)
     lane = lax.broadcasted_iota(jnp.int32, (orbitals, count * ATOMS), 1) // (2 * ATOMS)

time: 82.5 us -> 82.4 us (level)
  no operation moved by 1% of the time
where the time goes in v1:
time: 82.4 us; the launch traced here: 81.9 us
  blocking collectives  43.5 us (53%)
  Pallas kernels  15.9 us (19%)
  waiting for transfers between devices  13.2 us (16%)
  starting transfers between devices  8.63 us (10%)
    all_to_all x2, blocking collectives, shards(): gathered = lax.all_to_all(gradient, 'ao', 0, 0)  25.8 us
    all_to_all x2, blocking collectives, shards(): norms = lax.all_to_all(norms, 'orb', 0, 0)  17.7 us
    pallas_call x8, Pallas kernels, call(): pl.pallas_call(kernel, out_shape=out_shape, in_specs=specs or [HBM] * len...  15.9 us
    ppermute x1, waiting for transfers between devices, shards(): lax.ppermute(halfway, 'orb', [route for k in across for route in ((k + 4,...  7.98 us
    ppermute x4, starting transfers between devices, swap(): return lax.ppermute(block, 'orb', both_ways(pairs))  6.01 us
    ppermute x1, waiting for transfers between devices, shards(): lax.ppermute(odd_coeff, 'orb', [route for k in across for route in ((k, k...  5.17 us
  transfers between devices with their start and end apart: 6, of which 2 were waited for; matrix products, arithmetic and copies ran while one was open for 0% of the time, Pallas kernels for 7%

profile of v1, /device:TPU:0, one launch (start us, length us, event | category | flops | bytes accessed | tf_op | source)
XLA Modules:
  0.0 81.9 jit_solution(7082389607426370292)
XLA Ops:
  0.6 0.7 collective-permute-start
  1.4 4.6 %gradient.2 = (f32[4,112,128]{2,1,0:T(8,128)S(1)}, bf16[2,2,160,2176]{3,2,1,0:T(8,128)(2,1)S(1)}, bf16[2,2,160,2176]{3,2,1,0:T(8,128)(2,1)S(1)}) custom-call(s32[192,128]{1,0:T(8,128)} %atoms_hbm.3, s32[2,1,16]{2,1,0:T(1,128)} %list_hbm.1, f32[2,1280,128]{2,1,0:T(8,128)} %bitcast.10, f32[2,1280,128]{2,1,0:T(8,128)} %bitcast.8), custom_call_target="tpu_custom_call" | custom-call | tf_op jit(solution)/shard_map/gradient/pallas_call | solution.py:465
  6.0 13.1 %all_to_all.20.parts_ref = f32[4,112,128]{2,1,0:T(8,128)S(1)} all-to-all(f32[4,112,128]{2,1,0:T(8,128)S(1)} %get-tuple-element.22), channel_id=1, replica_groups=mesh['orb'=8,'ao'=4] {'ao'}, dimensions={0} | all-to-all | bytes 458752 | tf_op jit(solution)/shard_map/all_to_all | solution.py:505
  19.0 0.1 norm.2
  19.2 0.0 collective-permute-done.raw_hbm
  19.2 0.0 copy-start
  19.2 10.4 %all_to_all.21.refs_0_ = f32[8,8,128]{2,1,0:T(8,128)S(1)} all-to-all(f32[8,8,128]{2,1,0:T(8,128)S(1)} %get-tuple-element.24), channel_id=1, replica_groups=mesh['orb'=8,'ao'=4] {'orb'}, dimensions={0} | all-to-all | bytes 65536 | tf_op jit(solution)/shard_map/all_to_all | solution.py:518
  29.6 2.2 %rotation.2 = (f32[1288,128]{1,0:T(8,128)S(1)}, f32[1280,128]{1,0:T(8,128)S(1)}, f32[168,128]{1,0:T(8,128)S(1)}, bf16[2,160,160]{2,1,0:T(8,128)(2,1)S(1)}) custom-call(f32[8,8,128]{2,1,0:T(8,128)S(1)} %all_to_all.21.refs_0_, f32[112,128]{1,0:T(8,128)S(1)} %get-tuple-element.25.refs_1_, bf16[2,2,160,2176]{3,2,1,0:T(8,128)(2,1)S(1)} %get-tuple-element.26.refs_2_.data_high, ...), custom_call_target="tpu_custom_call" | custom-call | tf_op jit(solution)/shard_map/rotation/pallas_call | solution.py:465
  31.8 0.0 copy-done
  31.8 1.3 %collective-permute-start.4 = (f32[1288,128]{1,0:T(8,128)S(1)}, f32[1288,128]{1,0:T(8,128)S(1)}, u32[]{:S(2)}, u32[]{:S(2)}) collective-permute-start(f32[1288,128]{1,0:T(8,128)S(1)} %get-tuple-element.28.refs_0_), channel_id=1, source_target_pairs={{12,28},{16,0},{13,29},{17,1},{14,30},{18,2},{15,31},{19,3}} | collective-permute-start | bytes 1978376 | tf_op jit(solution)/shard_map/ppermute | solution.py:549
  33.1 0.7 collective-permute-start.1
  33.8 0.7 collective-permute-start.3
  34.5 0.0 collective-permute-done.1.turn_hbm
  34.5 0.7 later.1
  35.2 3.9 %collective-permute-start.2 = (f32[2568,128]{1,0:T(8,128)S(1)}, f32[2568,128]{1,0:T(8,128)S(1)}, u32[]{:S(2)}, u32[]{:S(2)}) collective-permute-start(f32[2568,128]{1,0:T(8,128)S(1)} %later.1), channel_id=1, source_target_pairs={{0,4},{4,0},{8,12},{12,8},{16,20},{20,16},{24,28},{28,24},{1,5},{5... | collective-permute-start | bytes 3944456 | tf_op jit(solution)/shard_map/ppermute | solution.py:446
  39.1 5.2 %collective-permute-done.4 = f32[1288,128]{1,0:T(8,128)S(1)} collective-permute-done((f32[1288,128]{1,0:T(8,128)S(1)}, f32[1288,128]{1,0:T(8,128)S(1)}, u32[]{:S(2)}, u32[]{:S(2)}) %collective-permute-start.4) | collective-permute-done | bytes 659488 | tf_op jit(solution)/shard_map/ppermute | solution.py:549
  44.3 1.3 %collective-permute-start.5 = (f32[1288,128]{1,0:T(8,128)S(1)}, f32[1288,128]{1,0:T(8,128)S(1)}, u32[]{:S(2)}, u32[]{:S(2)}) collective-permute-start(f32[1288,128]{1,0:T(8,128)S(1)} %collective-permute-done.4), channel_id=1, source_target_pairs={{28,16},{0,12},{29,17},{1,13},{30,18},{2,14},{31,19},{3,15}} | collective-permute-start | bytes 1978376 | tf_op jit(solution)/shard_map/ppermute | solution.py:568
  45.6 0.1 crossing.1.refs_5_
  45.7 0.0 collective-permute-done.3.refs_3_
  45.7 8.0 %collective-permute-done.5.refs_4_ = f32[1288,128]{1,0:T(8,128)S(1)} collective-permute-done((f32[1288,128]{1,0:T(8,128)S(1)}, f32[1288,128]{1,0:T(8,128)S(1)}, u32[]{:S(2)}, u32[]{:S(2)}) %collective-permute-start.5) | collective-permute-done | bytes 659488 | tf_op jit(solution)/shard_map/ppermute | solution.py:568
  53.7 0.0 collective-permute-done.2.refs_2_
  53.7 4.4 %gradient.3 = (f32[4,112,128]{2,1,0:T(8,128)S(1)}, bf16[2,2,160,2176]{3,2,1,0:T(8,128)(2,1)S(1)}, bf16[2,2,160,2176]{3,2,1,0:T(8,128)(2,1)S(1)}) custom-call(s32[192,128]{1,0:T(8,128)} %atoms_hbm.3, f32[1288,128]{1,0:T(8,128)S(1)} %get-tuple-element.28.refs_0_, f32[1280,128]{1,0:T(8,128)S(1)} %get-tuple-element.29.refs_1_, ...), custom_call_target="tpu_custom_call" | custom-call | tf_op jit(solution)/shard_map/gradient/pallas_call | solution.py:465
  58.2 12.7 %all_to_all.22.parts_ref = f32[4,112,128]{2,1,0:T(8,128)S(1)} all-to-all(f32[4,112,128]{2,1,0:T(8,128)S(1)} %get-tuple-element.35), channel_id=1, replica_groups=mesh['orb'=8,'ao'=4] {'ao'}, dimensions={0} | all-to-all | bytes 458752 | tf_op jit(solution)/shard_map/all_to_all | solution.py:505
  70.9 0.1 norm.3
  71.1 7.3 %all_to_all.23.refs_0_ = f32[8,8,128]{2,1,0:T(8,128)S(1)} all-to-all(f32[8,8,128]{2,1,0:T(8,128)S(1)} %get-tuple-element.36), channel_id=1, replica_groups=mesh['orb'=8,'ao'=4] {'orb'}, dimensions={0} | all-to-all | bytes 65536 | tf_op jit(solution)/shard_map/all_to_all | solution.py:518
  78.4 3.5 %rotation.3 = (f32[2,1280,128]{2,1,0:T(8,128)}, f32[2,1280,128]{2,1,0:T(8,128)}) custom-call(f32[8,8,128]{2,1,0:T(8,128)S(1)} %all_to_all.23.refs_0_, f32[112,128]{1,0:T(8,128)S(1)} %get-tuple-element.37.refs_1_, bf16[2,2,160,2176]{3,2,1,0:T(8,128)(2,1)S(1)} %get-tuple-element.38.refs_2_, bf16[2,2,160,2176]{3,2,1,0:T(8,128)(2,1)S(1)} %get-tuple-element.39.refs_3_), custom_call_target="tpu_custom_call" | custom-call | tf_op jit(solution)/shard_map/rotation/pallas_call | solution.py:465
Async XLA Ops:
  0.6 18.6 %collective-permute-start = (f32[2,1280,128]{2,1,0:T(8,128)}, f32[2,1280,128]{2,1,0:T(8,128)S(1)}, u32[]{:S(2)}, u32[]{:S(2)}) collective-permute-start(f32[2,1280,128]{2,1,0:T(8,128)} %bitcast.9), channel_id=1, source_target_pairs={{4,8},{8,4},{20,24},{24,20},{5,9},{9,5},{21,25},{25,21},{6,10},{10... | collective-permute-start | bytes 3932168 | tf_op jit(solution)/shard_map/ppermute | solution.py:446
  19.2 12.6 %copy-start = (f32[2,1280,128]{2,1,0:T(8,128)}, f32[2,1280,128]{2,1,0:T(8,128)S(1)}, u32[]{:S(2)}) copy-start(f32[2,1280,128]{2,1,0:T(8,128)S(1)} %collective-permute-done.raw_hbm) | copy-start | bytes 3932164
  31.8 12.5 %collective-permute-start.4 = (f32[1288,128]{1,0:T(8,128)S(1)}, f32[1288,128]{1,0:T(8,128)S(1)}, u32[]{:S(2)}, u32[]{:S(2)}) collective-permute-start(f32[1288,128]{1,0:T(8,128)S(1)} %get-tuple-element.28.refs_0_), channel_id=1, source_target_pairs={{12,28},{16,0},{13,29},{17,1},{14,30},{18,2},{15,31},{19,3}} | collective-permute-start | bytes 1978376 | tf_op jit(solution)/shard_map/ppermute | solution.py:549
  33.1 1.4 %collective-permute-start.1 = (f32[168,128]{1,0:T(8,128)S(1)}, f32[168,128]{1,0:T(8,128)S(1)}, u32[]{:S(2)}, u32[]{:S(2)}) collective-permute-start(f32[168,128]{1,0:T(8,128)S(1)} %get-tuple-element.31), channel_id=1, source_target_pairs={{4,8},{8,4},{20,24},{24,20},{5,9},{9,5},{21,25},{25,21},{6,10},{10... | collective-permute-start | bytes 258056 | tf_op jit(solution)/shard_map/ppermute | solution.py:446
  33.8 12.0 %collective-permute-start.3 = (f32[1280,128]{1,0:T(8,128)S(1)}, f32[1280,128]{1,0:T(8,128)S(1)}, u32[]{:S(2)}, u32[]{:S(2)}) collective-permute-start(f32[1280,128]{1,0:T(8,128)S(1)} %get-tuple-element.29.refs_1_), channel_id=1, source_target_pairs={{4,8},{8,4},{12,16},{16,12},{20,24},{24,20},{5,9},{9,5},{13,17},{1... | collective-permute-start | bytes 1966088 | tf_op jit(solution)/shard_map/ppermute | solution.py:446
  35.2 18.5 %collective-permute-start.2 = (f32[2568,128]{1,0:T(8,128)S(1)}, f32[2568,128]{1,0:T(8,128)S(1)}, u32[]{:S(2)}, u32[]{:S(2)}) collective-permute-start(f32[2568,128]{1,0:T(8,128)S(1)} %later.1), channel_id=1, source_target_pairs={{0,4},{4,0},{8,12},{12,8},{16,20},{20,16},{24,28},{28,24},{1,5},{5... | collective-permute-start | bytes 3944456 | tf_op jit(solution)/shard_map/ppermute | solution.py:446
  44.3 9.4 %collective-permute-start.5 = (f32[1288,128]{1,0:T(8,128)S(1)}, f32[1288,128]{1,0:T(8,128)S(1)}, u32[]{:S(2)}, u32[]{:S(2)}) collective-permute-start(f32[1288,128]{1,0:T(8,128)S(1)} %collective-permute-done.4), channel_id=1, source_target_pairs={{28,16},{0,12},{29,17},{1,13},{30,18},{2,14},{31,19},{3,15}} | collective-permute-start | bytes 1978376 | tf_op jit(solution)/shard_map/ppermute | solution.py:568
